TPU v7x, 256 devices: a whole 4x4x8 slice. The times are simulated.
256 devices in a mesh: ga: 32 (over y, z), ba: 8 (over x, core).
Axes of the slice: x: 4, y: 4, z: 8, core: 2. Of those that a mesh axis runs over, the one named last changes fastest.
Arguments:
- orbitals: bfloat16 [2, 512, 294912], P(None, 'ga', 'ba'), may hold values from -24 to 24, as said below
- exchange_applied: bfloat16 [2, 512, 294912], P(None, 'ga', 'ba'), may hold values from -48 to 48, as said below
Outputs:
- projectors: float32 [2, 512, 294912], P(None, None, ('ba', 'ga'))
Inputs may be any that keep to these rules, and one draw needn't show every extreme that they name: orbitals are bounded. exchange_applied is bounded and gram is positive definite.
All inputs are finite; a program needn't handle non-finite values.
Results may differ from a plain program's by a relative error of at most 0.0003.
Values may be sent and summed in bfloat16 or wider, within the bound.
A program may use at most 128 MiB of HBM per device.

v0:
```python
import jax
import jax.numpy as jnp
from jax import lax
from jax.sharding import PartitionSpec as P

NG = 294912


def local_correlation(orbit, applied):
    return jnp.einsum("sbg,scg->sbc", orbit, applied, preferred_element_type=jnp.float32)


def swapped(matrix):
    return jnp.swapaxes(matrix, 1, 2)


def invert_lower(lower):
    eye = jnp.eye(lower.shape[0], dtype=lower.dtype)
    return jax.scipy.linalg.solve_triangular(lower, eye, lower=True)


def per_device(orbitals, exchange_applied):
    orbit_slab, applied_slab = (
        lax.all_to_all(orbitals, "ga", split_axis=2, concat_axis=1, tiled=True),
        lax.all_to_all(exchange_applied, "ga", split_axis=2, concat_axis=1, tiled=True),
    )
    correlation = local_correlation(orbit_slab, applied_slab)
    total = lax.psum(correlation, ("ga", "ba"))
    sym = total + swapped(total)
    gram = -sym / (2.0 * NG)
    lower = jnp.linalg.cholesky(gram)
    inverse = jax.vmap(invert_lower)(lower)
    return jnp.einsum(
        "sbc,scg->sbg", inverse, applied_slab.astype(jnp.float32), precision=lax.Precision.HIGHEST
    )


def solution(mesh):
    placed = (P(None, "ga", "ba"), P(None, "ga", "ba"))
    return jax.shard_map(
        per_device,
        mesh=mesh,
        in_specs=placed,
        out_specs=P(None, None, ("ba", "ga")),
        check_vma=False,
    )
```

profile of v0, /device:TPU:1, one launch (start us, length us, event | category | flops | bytes accessed | tf_op | source)
XLA Modules:
  0.0 815.7 jit_solution(14717449357892092274)
XLA Ops:
  6.5 34.4 %copy.35 = bf16[2,16,36864]{1,0,2:T(2,128)(2,1)} copy(bf16[2,16,36864]{2,1,0:T(8,128)(2,1)} %param.3) | data formatting | bytes 4718592 | tf_op args[1]
  41.0 22.3 %reshape.75 = bf16[32,2,18432]{2,1,0:T(2,128)(2,1)} reshape(bf16[36864,2,16]{2,1,0:T(2,128)(2,1)} %bitcast.80) | data formatting | bytes 4718592
  63.2 12.0 %all-to-all-start.1 = ((bf16[32,2,18432]{2,1,0:T(2,128)(2,1)}), bf16[32,2,18432]{2,1,0:T(2,128)(2,1)S(1)}, u32[]{:S(2)}, u32[]{:S(2)}) async-start(bf16[32,2,18432]{2,1,0:T(2,128)(2,1)} %reshape.75), calls=%async_computation.1 | async-start | bytes 4718592 | tf_op jit(solution)/shard_map/all_to_all | solution.py:25
  75.3 34.4 %copy.33 = bf16[2,16,36864]{1,0,2:T(2,128)(2,1)} copy(bf16[2,16,36864]{2,1,0:T(8,128)(2,1)} %param.2) | data formatting | bytes 4718592 | tf_op args[0]
  109.7 22.2 %reshape.77 = bf16[32,2,18432]{2,1,0:T(2,128)(2,1)} reshape(bf16[36864,2,16]{2,1,0:T(2,128)(2,1)} %bitcast.81) | data formatting | bytes 4718592
  132.0 9.3 %all-to-all-start = ((bf16[32,2,18432]{2,1,0:T(2,128)(2,1)}), bf16[32,2,18432]{2,1,0:T(2,128)(2,1)}, u32[]{:S(2)}, u32[]{:S(2)}) async-start(bf16[32,2,18432]{2,1,0:T(2,128)(2,1)} %reshape.77), calls=%async_computation | async-start | bytes 4718592 | tf_op jit(solution)/shard_map/all_to_all | solution.py:24
  141.7 15.5 %reshape.76 = bf16[36864,2,16]{2,1,0:T(2,128)(2,1)} reshape(bf16[32,2,18432]{2,1,0:T(2,128)(2,1)S(1)} %all-to-all-done.1) | data formatting | bytes 4718592
  157.1 37.7 %copy.36 = bf16[2,16,32,1152]{3,1,2,0:T(8,128)(2,1)S(1)} copy(bf16[2,16,32,1152]{1,0,3,2:T(2,128)(2,1)} %bitcast.78) | data formatting | bytes 4718592 | tf_op jit(solution)/shard_map/all_to_all | solution.py:25
  195.9 17.5 %reshape.78 = bf16[36864,2,16]{2,1,0:T(2,128)(2,1)} reshape(bf16[32,2,18432]{2,1,0:T(2,128)(2,1)} %all-to-all-done) | data formatting | bytes 4718592
  213.4 38.4 %copy.34 = bf16[2,16,32,1152]{3,1,2,0:T(8,128)(2,1)} copy(bf16[2,16,32,1152]{1,0,3,2:T(2,128)(2,1)} %bitcast.79) | data formatting | bytes 4718592 | tf_op jit(solution)/shard_map/all_to_all | solution.py:24
  251.7 4.5 fusion.48
  258.6 258.6 %all-reduce.3.cloned.1.call-done = f32[2,512,512]{2,1,0:T(8,128)} async-done(((f32[2,512,512]{2,1,0:T(8,128)}), f32[2,512,512]{2,1,0:T(8,128)}) %all-reduce.3.cloned.1.call-update) | async-done | bytes 2097168 | tf_op jit(solution)/shard_map/psum | solution.py:28
  528.2 23.5 %custom-call.35 = f32[2,128,128]{2,1,0:T(8,128)S(1)} custom-call(f32[2,128,128]{2,1,0:T(8,128)S(1)} %cholesky.274), custom_call_target="Cholesky" | custom-call | tf_op jit(solution)/shard_map/jit(cholesky)/cholesky | solution.py:31
  551.7 19.7 %custom-call.36 = f32[2,1,128,128]{2,3,1,0:T(8,128)S(1)} custom-call(f32[2,1,128,128]{3,2,1,0:T(8,128)S(1)} %select_bitcast_fusion.2), custom_call_target="InvertDiagBlocksLowerTriangular" | custom-call | tf_op jit(solution)/shard_map/jit(cholesky)/cholesky | solution.py:31
  575.3 24.8 %custom-call.37 = f32[2,128,128]{2,1,0:T(8,128)S(1)} custom-call(f32[2,128,128]{2,1,0:T(8,128)} %cholesky.278), custom_call_target="Cholesky" | custom-call | tf_op jit(solution)/shard_map/jit(cholesky)/cholesky | solution.py:31
  600.7 21.1 %custom-call.38 = f32[2,1,128,128]{2,3,1,0:T(8,128)} custom-call(f32[2,1,128,128]{3,2,1,0:T(8,128)} %get-tuple-element.34), custom_call_target="InvertDiagBlocksLowerTriangular" | custom-call | tf_op jit(solution)/shard_map/jit(cholesky)/cholesky | solution.py:31
  625.4 24.3 %custom-call.39 = f32[2,128,128]{2,1,0:T(8,128)S(1)} custom-call(f32[2,128,128]{2,1,0:T(8,128)} %cholesky.283), custom_call_target="Cholesky" | custom-call | tf_op jit(solution)/shard_map/jit(cholesky)/cholesky | solution.py:31
  650.3 21.2 %custom-call.40 = f32[2,1,128,128]{2,3,1,0:T(8,128)} custom-call(f32[2,1,128,128]{3,2,1,0:T(8,128)} %get-tuple-element.32), custom_call_target="InvertDiagBlocksLowerTriangular" | custom-call | tf_op jit(solution)/shard_map/jit(cholesky)/cholesky | solution.py:31
  674.3 23.5 %custom-call.41 = f32[2,128,128]{2,1,0:T(8,128)S(1)} custom-call(f32[2,128,128]{2,1,0:T(8,128)S(1)} %convolution_subtract_fusion.4), custom_call_target="Cholesky" | custom-call | tf_op jit(solution)/shard_map/jit(cholesky)/cholesky | solution.py:31
  700.6 14.3 %while.1 = (s32[]{:T(128)}, f32[2,512,512]{2,1,0:T(8,128)}, s32[4,2]{0,1:T(2,128)S(1)}, f32[4,2,128,128]{3,2,0,1:T(8,128)}, s32[]{:T(128)}) while((s32[]{:T(128)}, f32[2,512,512]{2,1,0:T(8,128)}, s32[4,2]{0,1:T(2,128)S(1)}, f32[4,2,128,128]{3,2,0,1:T(8,128)}, s32[]{:T(128)}) %tuple.31), condition=%wide.while_cond, body=%wide.while_body.sunk | while | flops 2 | bytes 263777 | solution.py:19
  701.2 3.0 bitcast_dynamic-update-slice_fusion.2
  704.8 3.0 bitcast_dynamic-update-slice_fusion.2
  714.9 79.7 %custom-call.42 = f32[2,4,128,128]{2,3,1,0:T(8,128)S(1)} custom-call(f32[2,4,128,128]{3,2,1,0:T(8,128)} %bitcast.85), custom_call_target="InvertDiagBlocksLowerTriangular" | custom-call | tf_op jit(solution)/shard_map/vmap(jit(_solve_triangular))/triangular_solve | solution.py:19
  802.6 6.0 fusion
  (63 shorter events, 45.4 us)
Async XLA Ops:
  63.2 68.7 %all-to-all-start.1 = ((bf16[32,2,18432]{2,1,0:T(2,128)(2,1)}), bf16[32,2,18432]{2,1,0:T(2,128)(2,1)S(1)}, u32[]{:S(2)}, u32[]{:S(2)}) async-start(bf16[32,2,18432]{2,1,0:T(2,128)(2,1)} %reshape.75), calls=%async_computation.1 | async-start | bytes 4718592 | tf_op jit(solution)/shard_map/all_to_all | solution.py:25
  132.0 63.9 %all-to-all-start = ((bf16[32,2,18432]{2,1,0:T(2,128)(2,1)}), bf16[32,2,18432]{2,1,0:T(2,128)(2,1)}, u32[]{:S(2)}, u32[]{:S(2)}) async-start(bf16[32,2,18432]{2,1,0:T(2,128)(2,1)} %reshape.77), calls=%async_computation | async-start | bytes 4718592 | tf_op jit(solution)/shard_map/all_to_all | solution.py:24
  141.3 375.9 %all-reduce.3.cloned.1.call-start = ((), (), s32[]{:S(2)}) async-start(), calls=%async_computation.2 | async-start | bytes 4194304 | tf_op jit(solution)/shard_map/psum | solution.py:28
  194.8 56.9 %copy-start = (bf16[2,16,32,1152]{3,1,2,0:T(8,128)(2,1)}, bf16[2,16,32,1152]{3,1,2,0:T(8,128)(2,1)S(1)}, u32[]{:S(2)}) copy-start(bf16[2,16,32,1152]{3,1,2,0:T(8,128)(2,1)S(1)} %copy.36) | copy-start | bytes 7077892
  526.8 1.4 copy-start.2
  698.8 1.8 copy-start.5
  714.9 82.5 %copy-start.4 = (f32[128,512]{1,0:T(8,128)S(1)}, f32[128,512]{1,0:T(8,128)}, u32[]{:S(2)}) copy-start(f32[128,512]{1,0:T(8,128)} %get-tuple-element.28) | copy-start | bytes 786436
  796.7 3.0 copy-start.3
  799.7 2.9 copy-start.1
Sparse Core Ops, SparseCore 0:
  256.4 260.7 all-reduce.2
where the time goes:
time: 831 us; the launch traced here: 816 us
  waiting for transfers between devices  260 us (31%)
  other arithmetic  248 us (30%)
  local copies, waits for them, and re-layouts  245 us (29%)
  matrix products  27 us (3%)
  starting transfers between devices  21.7 us (3%)
  between operations  13.9 us (2%)
    psum x1, waiting for transfers between devices, per_device(): total = lax.psum(correlation, ('ga', 'ba'))  259 us
    another operation x16, other arithmetic, per_device(): lower = jnp.linalg.cholesky(gram)  161 us
    unnamed x18, local copies, waits for them, and re-layouts  148 us
    another operation x4, other arithmetic, invert_lower(): return jax.scipy.linalg.solve_triangular(lower, eye, lower=True)  82.1 us
    all_to_all x1, local copies, waits for them, and re-layouts, per_device(): lax.all_to_all(orbitals, 'ga', split_axis=2, concat_axis=1, tiled=True)  38.4 us
    all_to_all x1, local copies, waits for them, and re-layouts, per_device(): lax.all_to_all(exchange_applied, 'ga', split_axis=2, concat_axis=1, tiled...  37.7 us
  transfers between devices with their start and end apart: 3, of which 2 were waited for; matrix products, arithmetic and copies ran while one was open for 14% of the time, Pallas kernels for 0%

commit v1 on v0

v1 whole, which is shorter than its diff:
```python
import functools

import jax
import jax.numpy as jnp
from jax import lax
from jax.experimental import pallas as pl
from jax.experimental.pallas import tpu as pltpu
from jax.sharding import PartitionSpec as P

MESH = pl.DeviceIdType.MESH
HIGHEST = lax.Precision.HIGHEST
F32 = jnp.float32
BF16 = jnp.bfloat16
NB, NG, SETS = 512, 294912, 2
BLK = 128
NBLK = NB // BLK
PANEL = 16
PAIRS = [(i, j) for i in range(NBLK) for j in range(i, NBLK)]
FIRST = [PAIRS.index((i, i)) for i in range(NBLK)]
GROWS = len(PAIRS) * BLK
VMEM_LIMIT = 60 * 2**20
YS, ZS = 4, 8


def ring(d, n):
    return min(d, n - d)


OFFSETS = sorted(
    [(dy, dz) for dy in range(YS) for dz in range(ZS) if (dy, dz) != (0, 0)],
    key=lambda t: ring(t[0], YS) + ring(t[1], ZS),
)


def tn(a, b):
    return lax.dot_general(a, b, (((0,), (0,)), ((), ())), precision=HIGHEST, preferred_element_type=F32)


def nn(a, b):
    return lax.dot_general(a, b, (((1,), (0,)), ((), ())), precision=HIGHEST, preferred_element_type=F32)


def nt(a, b):
    return lax.dot_general(a, b, (((1,), (1,)), ((), ())), preferred_element_type=F32)


def factor_block(a_ref, x_ref):
    rows = lax.broadcasted_iota(jnp.int32, (BLK, BLK), 0)
    cols = lax.broadcasted_iota(jnp.int32, (BLK, BLK), 1)
    x_ref[...] = jnp.where(rows == cols, 1.0, 0.0).astype(F32)
    sub = lax.broadcasted_iota(jnp.int32, (8, BLK), 0)
    wide = (8, BLK)
    own = PANEL // 8
    for base in range(0, BLK, PANEL):
        v = own if base + PANEL == BLK else 2 * own
        a = [a_ref[base + 8 * i : base + 8 * i + 8, :] for i in range(v)]
        x = [x_ref[base + 8 * i : base + 8 * i + 8, :] for i in range(v)]
        c = [[jnp.broadcast_to(a[i][:, base + r : base + r + 1], wide) for i in range(v)] for r in range(PANEL)]
        d = [jnp.ones(wide, F32) for _ in range(own)]
        for r in range(PANEL):
            h, q = divmod(r, 8)
            pivot = jnp.broadcast_to(c[r][h][q : q + 1, :], wide)
            inv = 1.0 / pivot
            d[h] = jnp.where(sub == q, pivot, d[h])
            arow = jnp.broadcast_to(a[h][q : q + 1, :], wide)
            xrow = jnp.broadcast_to(x[h][q : q + 1, :], wide)
            crow = {j: jnp.broadcast_to(c[j][h][q : q + 1, :], wide) for j in range(r + 1, PANEL)}
            for i in range(h, v):
                if i == h and q == 7:
                    continue
                m = c[r][i] * inv
                if i == h:
                    m = jnp.where(sub > q, m, 0.0)
                for j in range(r + 1, PANEL):
                    c[j][i] = c[j][i] - m * crow[j]
                a[i] = a[i] - m * arow
                x[i] = x[i] - m * xrow
        for i in range(own):
            s = lax.rsqrt(d[i])
            a[i] = a[i] * s
            x[i] = x[i] * s
        for i in range(v):
            a_ref[base + 8 * i : base + 8 * i + 8, :] = a[i]
            x_ref[base + 8 * i : base + 8 * i + 8, :] = x[i]
        rest = base + 2 * PANEL
        if rest < BLK:
            u = a_ref[base : base + PANEL, :]
            w = x_ref[base : base + PANEL, :]
            a_ref[rest:, :] = a_ref[rest:, :] - tn(u, u)[rest:, :]
            x_ref[rest:, :] = x_ref[rest:, :] - tn(u, w)[rest:, :]


def factor(g_ref, x_ref, a_ref, m_ref, u_ref):
    def block(i, j):
        at = (FIRST[i] + j - i) * BLK
        return slice(at, at + BLK)

    x_ref[...] = jnp.zeros((NB, NB), F32)
    for k in range(NBLK):
        lo, hi = BLK * k, BLK * k + BLK
        a_ref[...] = g_ref[block(k, k), :]
        factor_block(a_ref, m_ref)
        m = m_ref[...]
        if k:
            x_ref[lo:hi, :lo] = nn(m, x_ref[lo:hi, :lo])
        x_ref[lo:hi, lo:hi] = m
        for j in range(k + 1, NBLK):
            u_ref[:, j * BLK : (j + 1) * BLK] = nn(m, g_ref[block(k, j), :])
        for i in range(k + 1, NBLK):
            li = BLK * i
            ui = u_ref[:, li : li + BLK]
            update = tn(ui, u_ref[:, li:])
            for j in range(i, NBLK):
                g_ref[block(i, j), :] = g_ref[block(i, j), :] - update[:, (j - i) * BLK : (j - i + 1) * BLK]
            x_ref[li : li + BLK, :hi] = x_ref[li : li + BLK, :hi] - tn(ui, x_ref[lo:hi, :hi])


def exchange_kernel(o_ref, w_ref, g_out, w_out, o_slab, send_sem, recv_sem, own_sem):
    ga, ba = lax.axis_index("ga"), lax.axis_index("ba")
    y, z = ga // ZS, lax.rem(ga, ZS)
    peers = [lax.rem(y + dy, YS) * ZS + lax.rem(z + dz, ZS) for dy, dz in OFFSETS]
    barrier = pltpu.get_barrier_semaphore()
    for p in peers:
        pl.semaphore_signal(barrier, inc=1, device_id=(p, ba), device_id_type=MESH)
    width = o_slab.shape[2]
    rows = o_ref.shape[1]
    mine = pl.ds(pl.multiple_of(ga * rows, rows), rows)
    own = pl.ds(pl.multiple_of(ga * width, BLK), width)
    arrays = ((o_ref, o_slab), (w_ref, w_out))
    local = [
        pltpu.make_async_copy(src.at[s, :, own], dst.at[s, mine, :], own_sem.at[s, a])
        for s in range(SETS)
        for a, (src, dst) in enumerate(arrays)
    ]
    for copy in local:
        copy.start()
    pl.semaphore_wait(barrier, len(peers))
    for s in range(SETS):
        for p in peers:
            columns = pl.ds(pl.multiple_of(p * width, BLK), width)
            for a, (src, dst) in enumerate(arrays):
                pltpu.make_async_remote_copy(
                    src_ref=src.at[s, :, columns],
                    dst_ref=dst.at[s, mine, :],
                    send_sem=send_sem.at[s, a],
                    recv_sem=recv_sem.at[s, a],
                    device_id=(p, ba),
                    device_id_type=MESH,
                ).start()
    for copy in local:
        copy.wait()
    for s in range(SETS):
        for a, (src, dst) in enumerate(arrays):
            all_but_one = dst.at[s, pl.ds(0, len(peers) * rows), :]
            pltpu.make_async_copy(all_but_one, all_but_one, recv_sem.at[s, a]).wait()
        for i in range(NBLK):
            lo = BLK * i
            product = nt(o_slab[s, lo : lo + BLK, :], w_out[s, lo:, :]) + nt(w_out[s, lo : lo + BLK, :], o_slab[s, lo:, :])
            for j in range(i, NBLK):
                at = (FIRST[i] + j - i) * BLK
                g_out[s, at : at + BLK, :] = product[:, (j - i) * BLK : (j - i + 1) * BLK] * (-0.5 / NG)
    for s in range(SETS):
        for a, (src, dst) in enumerate(arrays):
            all_but_one = dst.at[s, pl.ds(0, len(peers) * rows), :]
            pltpu.make_async_copy(all_but_one, all_but_one, send_sem.at[s, a]).wait()


def finish_kernel(g_ref, w_ref, out_ref, g, x, a, m, u):
    def one_set(s, carry):
        g[...] = g_ref[s]
        factor(g, x, a, m, u)
        for i in range(NBLK):
            lo, hi = BLK * i, BLK * i + BLK
            inverse = x[lo:hi, :hi]
            head = inverse.astype(BF16)
            tail = (inverse - head.astype(F32)).astype(BF16)
            slab = w_ref[s, :hi, :]
            out_ref[s, lo:hi, :] = jnp.dot(head, slab, preferred_element_type=F32) + jnp.dot(
                tail, slab, preferred_element_type=F32
            )
        return carry

    lax.fori_loop(0, SETS, one_set, 0)


def per_device(orbitals, exchange_applied):
    width = orbitals.shape[2] // (YS * ZS)
    vmem = pl.BlockSpec(memory_space=pltpu.VMEM)
    anywhere = pl.BlockSpec(memory_space=pl.ANY)
    gram, slab = pl.pallas_call(
        exchange_kernel,
        out_shape=(
            jax.ShapeDtypeStruct((SETS, GROWS, BLK), F32),
            jax.ShapeDtypeStruct((SETS, NB, width), BF16),
        ),
        in_specs=[anywhere, anywhere],
        out_specs=(vmem, vmem),
        scratch_shapes=[
            pltpu.VMEM((SETS, NB, width), BF16),
            pltpu.SemaphoreType.DMA((SETS, 2)),
            pltpu.SemaphoreType.DMA((SETS, 2)),
            pltpu.SemaphoreType.DMA((SETS, 2)),
        ],
        compiler_params=pltpu.CompilerParams(collective_id=0, has_side_effects=True, vmem_limit_bytes=VMEM_LIMIT),
    )(orbitals, exchange_applied)
    gram = lax.psum(gram, ("ga", "ba"))
    return pl.pallas_call(
        finish_kernel,
        out_shape=jax.ShapeDtypeStruct((SETS, NB, width), F32),
        in_specs=[vmem, vmem],
        out_specs=vmem,
        scratch_shapes=[
            pltpu.VMEM((GROWS, BLK), F32),
            pltpu.VMEM((NB, NB), F32),
            pltpu.VMEM((BLK, BLK), F32),
            pltpu.VMEM((BLK, BLK), F32),
            pltpu.VMEM((BLK, NB), F32),
        ],
        compiler_params=pltpu.CompilerParams(vmem_limit_bytes=VMEM_LIMIT),
    )(gram, slab)


def solution(mesh):
    placed = (P(None, "ga", "ba"), P(None, "ga", "ba"))
    return jax.shard_map(
        per_device,
        mesh=mesh,
        in_specs=placed,
        out_specs=P(None, None, ("ba", "ga")),
        check_vma=False,
    )
```

time: 831 us -> 426 us (0.51); the launches traced: 816 us -> 426 us
  other arithmetic: 248 us -> 0 us
  local copies, waits for them, and re-layouts: 245 us -> 0 us
  Pallas kernels: 0 us -> 151 us
  matrix products: 27 us -> 0 us
  starting transfers between devices: 21.7 us -> 0.01 us
    another operation x20 -> x0, other arithmetic: 243 us -> none  [the longest x16 161 us: per_device(): lower = jnp.linalg.cholesky(gram)]
    pallas_call x0 -> x2, Pallas kernels: none -> 151 us  [the longest x1 113 us: per_device(): pl.pallas_call(exchange_kernel, out_shape=(jax.ShapeDtypeStruct((SETS, GR...]
    unnamed x18 -> x0, local copies, waits for them, and re-layouts: 148 us -> none
    all_to_all x2 -> x0, local copies, waits for them, and re-layouts: 76 us -> none  [the longest x1 38.4 us: per_device(): lax.all_to_all(orbitals, 'ga', split_axis=2, concat_axis=1, tiled=True)]
    all_to_all x2 -> x0, starting transfers between devices: 21.4 us -> none  [the longest x1 12 us: per_device(): lax.all_to_all(exchange_applied, 'ga', split_axis=2, concat_axis=1, tiled...]
    another operation x18 -> x0, local copies, waits for them, and re-layouts: 16.8 us -> none
    another operation x13 -> x0, matrix products: 16.5 us -> none  [the longest x6 8.53 us: per_device(): lower = jnp.linalg.cholesky(gram)]
    dot_general x2 -> x0, matrix products: 10.5 us -> none  [the longest x1 6 us: per_device(): jnp.einsum('sbc,scg->sbg', inverse, applied_slab.astype(jnp.float32), pre...]
  transfers between devices with their start and end apart: 3 -> 1, of which waited for: 2 -> 1; matrix products, arithmetic and copies ran while one was open for 14% -> 0% of each run, Pallas kernels for 0% -> 0%
where the time goes in v1:
time: 426 us
  waiting for transfers between devices  262 us (62%)
  Pallas kernels  151 us (35%)
  between operations  13.4 us (3%)
    psum x1, waiting for transfers between devices, per_device(): gram = lax.psum(gram, ('ga', 'ba'))  261 us
    pallas_call x1, Pallas kernels, per_device(): pl.pallas_call(exchange_kernel, out_shape=(jax.ShapeDtypeStruct((SETS, GR...  113 us
    pallas_call x1, Pallas kernels, per_device(): pl.pallas_call(finish_kernel, out_shape=jax.ShapeDtypeStruct((SETS, NB, w...  37.4 us
  transfers between devices with their start and end apart: 1, of which 1 were waited for; matrix products, arithmetic and copies ran while one was open for 0% of the time, Pallas kernels for 0%

profile of v1, /device:TPU:1, one launch (start us, length us, event | category | flops | bytes accessed | tf_op | source)
XLA Modules:
  0.0 425.7 jit_solution(9534426564293139178)
XLA Ops:
  6.5 0.0 all-reduce.2.cloned.1.call-start
  6.5 113.4 %shard_map.28 = (f32[2,1280,128]{2,1,0:T(8,128)}, bf16[2,512,1152]{2,1,0:T(8,128)(2,1)}) custom-call(bf16[2,16,36864]{2,1,0:T(8,128)(2,1)} %o_ref.1, bf16[2,16,36864]{2,1,0:T(8,128)(2,1)} %w_ref.1), custom_call_target="tpu_custom_call" | custom-call | tf_op jit(solution)/shard_map/pallas_call | solution.py:190
  120.0 0.0 all-reduce.2.cloned.1.call-update
  120.0 261.5 %all-reduce.2.cloned.1.call-done.g_ref = f32[2,1280,128]{2,1,0:T(8,128)} async-done(((f32[2,1280,128]{2,1,0:T(8,128)}), f32[2,1280,128]{2,1,0:T(8,128)}) %all-reduce.2.cloned.1.call-update) | async-done | bytes 1310736 | tf_op jit(solution)/shard_map/psum | solution.py:206
  381.5 37.4 %shard_map.29 = f32[2,512,1152]{2,1,0:T(8,128)} custom-call(f32[2,1280,128]{2,1,0:T(8,128)} %all-reduce.2.cloned.1.call-done.g_ref, bf16[2,512,1152]{2,1,0:T(8,128)(2,1)} %get-tuple-element.8.w_ref), custom_call_target="tpu_custom_call" | custom-call | tf_op jit(solution)/shard_map/pallas_call | solution.py:207
Async XLA Ops:
  6.5 375.0 %all-reduce.2.cloned.1.call-start = ((), (), s32[]{:S(2)}) async-start(), calls=%async_computation | async-start | bytes 2621440 | tf_op jit(solution)/shard_map/psum | solution.py:206
Sparse Core Ops, SparseCore 0:
  120.1 261.3 all-reduce.1

commit v2 on v1

--- a/solution.py
+++ b/solution.py
@@ -17,10 +17,12 @@
 PANEL = 16
 PAIRS = [(i, j) for i in range(NBLK) for j in range(i, NBLK)]
 FIRST = [PAIRS.index((i, i)) for i in range(NBLK)]
-GROWS = len(PAIRS) * BLK
+GROWS = 12 * BLK
+XS, YS, ZS = 4, 4, 8
+HALF = GROWS // 2
+PART = HALF // 2 // XS
+CHUNK = 2 * PART // ZS
 VMEM_LIMIT = 60 * 2**20
-YS, ZS = 4, 8
-
 
 def ring(d, n):
     return min(d, n - d)
@@ -115,13 +117,25 @@
             x_ref[li : li + BLK, :hi] = x_ref[li : li + BLK, :hi] - tn(ui, x_ref[lo:hi, :hi])
 
 
-def exchange_kernel(o_ref, w_ref, g_out, w_out, o_slab, send_sem, recv_sem, own_sem):
+def exchange_kernel(
+    o_ref, w_ref, g_out, w_out, o_slab, part, half, from_x, from_y, third, from_z, fourth, from_4, send_sem, recv_sem, own_sem, out_sem, in_sem
+):
     ga, ba = lax.axis_index("ga"), lax.axis_index("ba")
     y, z = ga // ZS, lax.rem(ga, ZS)
-    peers = [lax.rem(y + dy, YS) * ZS + lax.rem(z + dz, ZS) for dy, dz in OFFSETS]
+    x, core = ba // 2, lax.rem(ba, 2)
+
+    def device(x, y, z, core):
+        return (y * ZS + z, x * 2 + core)
+
+    def ahead(i, k, n):
+        return lax.rem(i + k, n)
+
+    peers = [device(x, ahead(y, dy, YS), ahead(z, dz, ZS), core) for dy, dz in OFFSETS]
+    partner = device(x, y, z, 1 - core)
+    beside = [device(ahead(x, k, XS), y, z, core) for k in range(1, XS)]
     barrier = pltpu.get_barrier_semaphore()
-    for p in peers:
-        pl.semaphore_signal(barrier, inc=1, device_id=(p, ba), device_id_type=MESH)
+    for p in [*peers, partner, *beside]:
+        pl.semaphore_signal(barrier, inc=1, device_id=p, device_id_type=MESH)
     width = o_slab.shape[2]
     rows = o_ref.shape[1]
     mine = pl.ds(pl.multiple_of(ga * rows, rows), rows)
@@ -134,35 +148,114 @@
     ]
     for copy in local:
         copy.start()
-    pl.semaphore_wait(barrier, len(peers))
-    for s in range(SETS):
-        for p in peers:
-            columns = pl.ds(pl.multiple_of(p * width, BLK), width)
+    part[:, len(PAIRS) * BLK :, :] = jnp.zeros((SETS, GROWS - len(PAIRS) * BLK, BLK), F32)
+    pl.semaphore_wait(barrier, len(peers) + 1 + len(beside))
+
+    def send_slabs(s, chosen):
+        for p in chosen:
+            columns = pl.ds(pl.multiple_of(p[0] * width, BLK), width)
             for a, (src, dst) in enumerate(arrays):
                 pltpu.make_async_remote_copy(
                     src_ref=src.at[s, :, columns],
                     dst_ref=dst.at[s, mine, :],
                     send_sem=send_sem.at[s, a],
                     recv_sem=recv_sem.at[s, a],
-                    device_id=(p, ba),
+                    device_id=p,
                     device_id_type=MESH,
                 ).start()
-    for copy in local:
-        copy.wait()
-    for s in range(SETS):
+
+    def wait_slabs(s, sem):
         for a, (src, dst) in enumerate(arrays):
             all_but_one = dst.at[s, pl.ds(0, len(peers) * rows), :]
-            pltpu.make_async_copy(all_but_one, all_but_one, recv_sem.at[s, a]).wait()
+            pltpu.make_async_copy(all_but_one, all_but_one, sem.at[s, a]).wait()
+
+    def correlate(s):
         for i in range(NBLK):
             lo = BLK * i
             product = nt(o_slab[s, lo : lo + BLK, :], w_out[s, lo:, :]) + nt(w_out[s, lo : lo + BLK, :], o_slab[s, lo:, :])
             for j in range(i, NBLK):
                 at = (FIRST[i] + j - i) * BLK
-                g_out[s, at : at + BLK, :] = product[:, (j - i) * BLK : (j - i + 1) * BLK] * (-0.5 / NG)
+                part[s, at : at + BLK, :] = product[:, (j - i) * BLK : (j - i + 1) * BLK] * (-0.5 / NG)
+
+    def span(start, size):
+        return pl.ds(pl.multiple_of(start, 8), size)
+
+    def total(s, between):
+        used = []
+
+        def stage(t, transfers):
+            copies = []
+            for src, dst, to in transfers:
+                at = len(used) + len(copies)
+                copies.append(
+                    pltpu.make_async_remote_copy(
+                        src_ref=src, dst_ref=dst, send_sem=out_sem.at[s, at], recv_sem=in_sem.at[s, at], device_id=to, device_id_type=MESH
+                    )
+                )
+            for copy in copies:
+                copy.start()
+            between(t)
+            for copy in copies:
+                copy.wait_recv()
+            used.extend(copies)
+
+        stage(0, [(part.at[s, span((1 - core) * HALF, HALF), :], half.at[s], partner)])
+        half[s] = half[s] + part[s, span(core * HALF, HALF), :]
+        side = HALF // 2
+        xs = [ahead(x, k, XS) for k in range(1, XS)]
+        ys = [ahead(y, k, YS) for k in range(1, YS)]
+        zs = [ahead(z, k, ZS) for k in range(1, ZS)]
+        stage(
+            1,
+            [(half.at[s, span(xx * PART, PART), :], from_x.at[s, k], device(xx, y, z, core)) for k, xx in enumerate(xs)]
+            + [(half.at[s, span(side + yy * PART, PART), :], from_y.at[s, k], device(x, yy, z, core)) for k, yy in enumerate(ys)],
+        )
+        third[s, :PART, :] = half[s, span(x * PART, PART), :] + (from_x[s, 0] + from_x[s, 1] + from_x[s, 2])
+        third[s, PART:, :] = half[s, span(side + y * PART, PART), :] + (from_y[s, 0] + from_y[s, 1] + from_y[s, 2])
+        stage(2, [(third.at[s, span(zz * CHUNK, CHUNK), :], from_z.at[s, k], device(x, y, zz, core)) for k, zz in enumerate(zs)])
+        got = [from_z[s, k] for k in range(ZS - 1)]
+        fourth[s] = third[s, span(z * CHUNK, CHUNK), :] + (
+            ((got[0] + got[1]) + (got[2] + got[3])) + ((got[4] + got[5]) + got[6])
+        )
+        upper = z // (ZS // 2)
+        stage(
+            3,
+            [
+                (fourth.at[s], from_4.at[s, k - 1], device(ahead(x, k * upper, XS), ahead(y, k * (1 - upper), YS), z, core))
+                for k in range(1, 4)
+            ],
+        )
+        start_x = core * HALF + x * PART
+        start_y = core * HALF + side + y * PART
+        start = (1 - upper) * (start_x + z * CHUNK) + upper * (start_y + (z - ZS // 2) * CHUNK)
+        g_out[s, span(start, CHUNK), :] = fourth[s] + (from_4[s, 0] + from_4[s, 1] + from_4[s, 2])
+        here = g_out.at[s, span(start, CHUNK), :]
+        stage(4, [(here, here, device(x, y, zz, core)) for zz in zs])
+        along_x = g_out.at[s, span(start_x, PART), :]
+        along_y = g_out.at[s, span(start_y, PART), :]
+        stage(
+            5,
+            [(along_x, along_x, device(xx, y, z, core)) for xx in xs] + [(along_y, along_y, device(x, yy, z, core)) for yy in ys],
+        )
+        share = g_out.at[s, span(core * HALF, HALF), :]
+        stage(6, [(share, share, partner)])
+        return used
+
+    batches = [peers[i::8] for i in range(8)]
+    send_slabs(0, peers)
+    send_slabs(1, batches[0])
+    for copy in local:
+        copy.wait()
+    wait_slabs(0, recv_sem)
+    correlate(0)
+    used = total(0, lambda t: send_slabs(1, batches[t + 1]))
+    wait_slabs(1, recv_sem)
+    correlate(1)
+    used = used + total(1, lambda t: None)
+    for copy in used:
+        copy.wait_send()
     for s in range(SETS):
-        for a, (src, dst) in enumerate(arrays):
-            all_but_one = dst.at[s, pl.ds(0, len(peers) * rows), :]
-            pltpu.make_async_copy(all_but_one, all_but_one, send_sem.at[s, a]).wait()
+        wait_slabs(s, send_sem)
 
 
 def finish_kernel(g_ref, w_ref, out_ref, g, x, a, m, u):
@@ -197,13 +290,22 @@
         out_specs=(vmem, vmem),
         scratch_shapes=[
             pltpu.VMEM((SETS, NB, width), BF16),
+            pltpu.VMEM((SETS, GROWS, BLK), F32),
+            pltpu.VMEM((SETS, HALF, BLK), F32),
+            pltpu.VMEM((SETS, XS - 1, PART, BLK), F32),
+            pltpu.VMEM((SETS, YS - 1, PART, BLK), F32),
+            pltpu.VMEM((SETS, 2 * PART, BLK), F32),
+            pltpu.VMEM((SETS, ZS - 1, CHUNK, BLK), F32),
+            pltpu.VMEM((SETS, CHUNK, BLK), F32),
+            pltpu.VMEM((SETS, 3, CHUNK, BLK), F32),
             pltpu.SemaphoreType.DMA((SETS, 2)),
             pltpu.SemaphoreType.DMA((SETS, 2)),
             pltpu.SemaphoreType.DMA((SETS, 2)),
+            pltpu.SemaphoreType.DMA((SETS, 31)),
+            pltpu.SemaphoreType.DMA((SETS, 31)),
         ],
         compiler_params=pltpu.CompilerParams(collective_id=0, has_side_effects=True, vmem_limit_bytes=VMEM_LIMIT),
     )(orbitals, exchange_applied)
-    gram = lax.psum(gram, ("ga", "ba"))
     return pl.pallas_call(
         finish_kernel,
         out_shape=jax.ShapeDtypeStruct((SETS, NB, width), F32),

time: 426 us -> 198 us (0.46)
  waiting for transfers between devices: 262 us -> 0 us
  Pallas kernels: 151 us -> 198 us
  between operations: 13.4 us -> 0.01 us
    psum x1 -> x0, waiting for transfers between devices: 261 us -> none  [per_device(): gram = lax.psum(gram, ('ga', 'ba'))]
    pallas_call x1, Pallas kernels: 113 us -> 161 us  [per_device(): pl.pallas_call(exchange_kernel, out_shape=(jax.ShapeDtypeStruct((SETS, GR...]
  transfers between devices with their start and end apart: 1 -> 0, of which waited for: 1 -> 0; matrix products, arithmetic and copies ran while one was open for 0% -> 0% of each run, Pallas kernels for 0% -> 0%
where the time goes in v2:
time: 198 us
  Pallas kernels  198 us (100%)
    pallas_call x1, Pallas kernels, per_device(): pl.pallas_call(exchange_kernel, out_shape=(jax.ShapeDtypeStruct((SETS, GR...  161 us
    pallas_call x1, Pallas kernels, per_device(): pl.pallas_call(finish_kernel, out_shape=jax.ShapeDtypeStruct((SETS, NB, w...  37.4 us

profile of v2, /device:TPU:1, one launch (start us, length us, event | category | flops | bytes accessed | tf_op | source)
XLA Modules:
  0.0 198.2 jit_solution(12497200533948478780)
XLA Ops:
  0.0 160.7 %shard_map.28 = (f32[2,1536,128]{2,1,0:T(8,128)}, bf16[2,512,1152]{2,1,0:T(8,128)(2,1)}) custom-call(bf16[2,16,36864]{2,1,0:T(8,128)(2,1)} %o_ref.1, bf16[2,16,36864]{2,1,0:T(8,128)(2,1)} %w_ref.1), custom_call_target="tpu_custom_call" | custom-call | tf_op jit(solution)/shard_map/pallas_call | solution.py:283
  160.7 37.4 %shard_map.29 = f32[2,512,1152]{2,1,0:T(8,128)} custom-call(f32[2,1536,128]{2,1,0:T(8,128)} %get-tuple-element.7.g_ref, bf16[2,512,1152]{2,1,0:T(8,128)(2,1)} %get-tuple-element.8.w_ref), custom_call_target="tpu_custom_call" | custom-call | tf_op jit(solution)/shard_map/pallas_call | solution.py:309

commit v3 on v2

--- a/solution.py
+++ b/solution.py
@@ -13,6 +13,7 @@
 BF16 = jnp.bfloat16
 NB, NG, SETS = 512, 294912, 2
 BLK = 128
+HB = BLK // 2
 NBLK = NB // BLK
 PANEL = 16
 PAIRS = [(i, j) for i in range(NBLK) for j in range(i, NBLK)]
@@ -46,26 +47,49 @@
     return lax.dot_general(a, b, (((1,), (1,)), ((), ())), preferred_element_type=F32)
 
 
-def factor_block(a_ref, x_ref):
-    rows = lax.broadcasted_iota(jnp.int32, (BLK, BLK), 0)
-    cols = lax.broadcasted_iota(jnp.int32, (BLK, BLK), 1)
-    x_ref[...] = jnp.where(rows == cols, 1.0, 0.0).astype(F32)
-    sub = lax.broadcasted_iota(jnp.int32, (8, BLK), 0)
+def pack(first, second):
+    return jnp.concatenate([first[:, :HB], second[:, :HB], first[:, HB:], second[:, HB:]], axis=1)
+
+
+def unpack(packed):
+    return (
+        jnp.concatenate([packed[:, :HB], packed[:, BLK : BLK + HB]], axis=1),
+        jnp.concatenate([packed[:, HB:BLK], packed[:, BLK + HB :]], axis=1),
+    )
+
+
+def factor_blocks(a_ref, x_ref):
     wide = (8, BLK)
+    sub = lax.broadcasted_iota(jnp.int32, wide, 0)
+    left = lax.broadcasted_iota(jnp.int32, wide, 1) < HB
+    rows = lax.broadcasted_iota(jnp.int32, (BLK, 2 * BLK), 0)
+    cols = lax.broadcasted_iota(jnp.int32, (BLK, 2 * BLK), 1)
+    x_ref[...] = jnp.where(rows == cols % HB + cols // BLK * HB, 1.0, 0.0).astype(F32)
     own = PANEL // 8
     for base in range(0, BLK, PANEL):
         v = own if base + PANEL == BLK else 2 * own
-        a = [a_ref[base + 8 * i : base + 8 * i + 8, :] for i in range(v)]
-        x = [x_ref[base + 8 * i : base + 8 * i + 8, :] for i in range(v)]
-        c = [[jnp.broadcast_to(a[i][:, base + r : base + r + 1], wide) for i in range(v)] for r in range(PANEL)]
+        at = [slice(base + 8 * i, base + 8 * i + 8) for i in range(v)]
+        t = [[a_ref[at[i], :BLK], a_ref[at[i], BLK:], x_ref[at[i], :BLK], x_ref[at[i], BLK:]] for i in range(v)]
+        side, first = divmod(base, HB)
+        c = [
+            [
+                jnp.where(
+                    left,
+                    jnp.broadcast_to(t[i][side][:, first + r : first + r + 1], wide),
+                    jnp.broadcast_to(t[i][side][:, HB + first + r : HB + first + r + 1], wide),
+                )
+                for i in range(v)
+            ]
+            for r in range(PANEL)
+        ]
+        live = [k for k in range(4) if not (k == 0 and side == 1) and not (k == 3 and side == 0 and base + 2 * PANEL <= HB)]
         d = [jnp.ones(wide, F32) for _ in range(own)]
         for r in range(PANEL):
             h, q = divmod(r, 8)
             pivot = jnp.broadcast_to(c[r][h][q : q + 1, :], wide)
             inv = 1.0 / pivot
             d[h] = jnp.where(sub == q, pivot, d[h])
-            arow = jnp.broadcast_to(a[h][q : q + 1, :], wide)
-            xrow = jnp.broadcast_to(x[h][q : q + 1, :], wide)
+            trow = {k: jnp.broadcast_to(t[h][k][q : q + 1, :], wide) for k in live}
             crow = {j: jnp.broadcast_to(c[j][h][q : q + 1, :], wide) for j in range(r + 1, PANEL)}
             for i in range(h, v):
                 if i == h and q == 7:
@@ -75,21 +99,30 @@
                     m = jnp.where(sub > q, m, 0.0)
                 for j in range(r + 1, PANEL):
                     c[j][i] = c[j][i] - m * crow[j]
-                a[i] = a[i] - m * arow
-                x[i] = x[i] - m * xrow
+                for k in live:
+                    t[i][k] = t[i][k] - m * trow[k]
         for i in range(own):
             s = lax.rsqrt(d[i])
-            a[i] = a[i] * s
-            x[i] = x[i] * s
+            t[i] = [e * s for e in t[i]]
         for i in range(v):
-            a_ref[base + 8 * i : base + 8 * i + 8, :] = a[i]
-            x_ref[base + 8 * i : base + 8 * i + 8, :] = x[i]
+            a_ref[at[i], :BLK], a_ref[at[i], BLK:], x_ref[at[i], :BLK], x_ref[at[i], BLK:] = t[i]
         rest = base + 2 * PANEL
         if rest < BLK:
             u = a_ref[base : base + PANEL, :]
             w = x_ref[base : base + PANEL, :]
-            a_ref[rest:, :] = a_ref[rest:, :] - tn(u, u)[rest:, :]
-            x_ref[rest:, :] = x_ref[rest:, :] - tn(u, w)[rest:, :]
+            both = jnp.concatenate([u, w], axis=1)
+            for lo in (0, HB):
+                if rest >= lo + HB:
+                    continue
+                skip = max(rest - lo, 0)
+                p = tn(u[:, 2 * lo : 2 * lo + BLK], both)
+                pick = lax.broadcasted_iota(jnp.int32, (HB - skip, 4 * BLK), 1) % BLK < HB
+                update = jnp.where(pick, p[skip:HB], p[HB + skip :])
+                if lo == 0 or rest <= HB:
+                    a_ref[lo + skip : lo + HB, :] = a_ref[lo + skip : lo + HB, :] - update[:, : 2 * BLK]
+                else:
+                    a_ref[lo + skip : lo + HB, BLK:] = a_ref[lo + skip : lo + HB, BLK:] - update[:, BLK : 2 * BLK]
+                x_ref[lo + skip : lo + HB, :] = x_ref[lo + skip : lo + HB, :] - update[:, 2 * BLK :]
 
 
 def factor(g_ref, x_ref, a_ref, m_ref, u_ref):
@@ -97,28 +130,38 @@
         at = (FIRST[i] + j - i) * BLK
         return slice(at, at + BLK)
 
-    x_ref[...] = jnp.zeros((NB, NB), F32)
-    for k in range(NBLK):
-        lo, hi = BLK * k, BLK * k + BLK
-        a_ref[...] = g_ref[block(k, k), :]
-        factor_block(a_ref, m_ref)
-        m = m_ref[...]
-        if k:
-            x_ref[lo:hi, :lo] = nn(m, x_ref[lo:hi, :lo])
-        x_ref[lo:hi, lo:hi] = m
-        for j in range(k + 1, NBLK):
-            u_ref[:, j * BLK : (j + 1) * BLK] = nn(m, g_ref[block(k, j), :])
-        for i in range(k + 1, NBLK):
-            li = BLK * i
-            ui = u_ref[:, li : li + BLK]
-            update = tn(ui, u_ref[:, li:])
-            for j in range(i, NBLK):
-                g_ref[block(i, j), :] = g_ref[block(i, j), :] - update[:, (j - i) * BLK : (j - i + 1) * BLK]
-            x_ref[li : li + BLK, :hi] = x_ref[li : li + BLK, :hi] - tn(ui, x_ref[lo:hi, :hi])
+    x_ref[...] = jnp.zeros((SETS, NB, NB), F32)
+
+    def step(k, carry):
+        diagonal = pl.ds(pl.multiple_of(k * (2 * NBLK + 1 - k) // 2 * BLK, BLK), BLK)
+        a_ref[...] = pack(g_ref[0, diagonal, :], g_ref[1, diagonal, :])
+        factor_blocks(a_ref, m_ref)
+        ms = unpack(m_ref[...])
+        for kk in range(NBLK):
+            @pl.when(k == kk)
+            def _():
+                lo, hi = BLK * kk, BLK * kk + BLK
+                for s, m in enumerate(ms):
+                    if kk:
+                        x_ref[s, lo:hi, :lo] = nn(m, x_ref[s, lo:hi, :lo])
+                    x_ref[s, lo:hi, lo:hi] = m
+                    for j in range(kk + 1, NBLK):
+                        u_ref[s, :, j * BLK : (j + 1) * BLK] = nn(m, g_ref[s, block(kk, j), :])
+                for s, m in enumerate(ms):
+                    for i in range(kk + 1, NBLK):
+                        li = BLK * i
+                        ui = u_ref[s, :, li : li + BLK]
+                        update = tn(ui, u_ref[s, :, li:])
+                        for j in range(i, NBLK):
+                            g_ref[s, block(i, j), :] = g_ref[s, block(i, j), :] - update[:, (j - i) * BLK : (j - i + 1) * BLK]
+                        x_ref[s, li : li + BLK, :hi] = x_ref[s, li : li + BLK, :hi] - tn(ui, x_ref[s, lo:hi, :hi])
+        return carry
+
+    lax.fori_loop(0, NBLK, step, 0)
 
 
 def exchange_kernel(
-    o_ref, w_ref, g_out, w_out, o_slab, part, half, from_x, from_y, third, from_z, fourth, from_4, send_sem, recv_sem, own_sem, out_sem, in_sem
+    o_ref, w_ref, g_out, w_out, o_slab, w_slab, part, half, from_x, from_y, third, from_z, fourth, from_4, send_sem, recv_sem, own_sem, out_sem, in_sem, keep_sem
 ):
     ga, ba = lax.axis_index("ga"), lax.axis_index("ba")
     y, z = ga // ZS, lax.rem(ga, ZS)
@@ -140,7 +183,7 @@
     rows = o_ref.shape[1]
     mine = pl.ds(pl.multiple_of(ga * rows, rows), rows)
     own = pl.ds(pl.multiple_of(ga * width, BLK), width)
-    arrays = ((o_ref, o_slab), (w_ref, w_out))
+    arrays = ((o_ref, o_slab), (w_ref, w_slab))
     local = [
         pltpu.make_async_copy(src.at[s, :, own], dst.at[s, mine, :], own_sem.at[s, a])
         for s in range(SETS)
@@ -172,7 +215,7 @@
     def correlate(s):
         for i in range(NBLK):
             lo = BLK * i
-            product = nt(o_slab[s, lo : lo + BLK, :], w_out[s, lo:, :]) + nt(w_out[s, lo : lo + BLK, :], o_slab[s, lo:, :])
+            product = nt(o_slab[s, lo : lo + BLK, :], w_slab[s, lo:, :]) + nt(w_slab[s, lo : lo + BLK, :], o_slab[s, lo:, :])
             for j in range(i, NBLK):
                 at = (FIRST[i] + j - i) * BLK
                 part[s, at : at + BLK, :] = product[:, (j - i) * BLK : (j - i + 1) * BLK] * (-0.5 / NG)
@@ -241,39 +284,51 @@
         stage(6, [(share, share, partner)])
         return used
 
-    batches = [peers[i::8] for i in range(8)]
+    cuts = [0, 12, 16, 20, 24, 28, 31, 31, 31]
+    batches = [peers[i:j] for i, j in zip(cuts, cuts[1:])]
     send_slabs(0, peers)
     send_slabs(1, batches[0])
     for copy in local:
         copy.wait()
     wait_slabs(0, recv_sem)
+    keep = [pltpu.make_async_copy(w_slab.at[s], w_out.at[s], keep_sem.at[s]) for s in range(SETS)]
+    keep[0].start()
     correlate(0)
     used = total(0, lambda t: send_slabs(1, batches[t + 1]))
     wait_slabs(1, recv_sem)
+    keep[1].start()
     correlate(1)
     used = used + total(1, lambda t: None)
     for copy in used:
         copy.wait_send()
+    for copy in keep:
+        copy.wait()
     for s in range(SETS):
         wait_slabs(s, send_sem)
 
 
-def finish_kernel(g_ref, w_ref, out_ref, g, x, a, m, u):
-    def one_set(s, carry):
-        g[...] = g_ref[s]
-        factor(g, x, a, m, u)
+def finish_kernel(g_ref, w_ref, out_ref, g, x, a, m, u, slab, result, in_sem, out_sem):
+    fetch = pltpu.make_async_copy(w_ref, slab, in_sem)
+    fetch.start()
+    g[...] = g_ref[...]
+    factor(g, x, a, m, u)
+    fetch.wait()
+    stores = []
+    for s in range(SETS):
         for i in range(NBLK):
             lo, hi = BLK * i, BLK * i + BLK
-            inverse = x[lo:hi, :hi]
+            inverse = x[s, lo:hi, :hi]
             head = inverse.astype(BF16)
             tail = (inverse - head.astype(F32)).astype(BF16)
-            slab = w_ref[s, :hi, :]
-            out_ref[s, lo:hi, :] = jnp.dot(head, slab, preferred_element_type=F32) + jnp.dot(
-                tail, slab, preferred_element_type=F32
+            known = slab[s, :hi, :]
+            result[s, lo:hi, :] = jnp.dot(head, known, preferred_element_type=F32) + jnp.dot(
+                tail, known, preferred_element_type=F32
             )
-        return carry
-
-    lax.fori_loop(0, SETS, one_set, 0)
+            here = result.at[s, pl.ds(lo, BLK), :]
+            stores.append(pltpu.make_async_copy(here, out_ref.at[s, pl.ds(lo, BLK), :], out_sem.at[s, i]))
+            stores[-1].start()
+    for store in stores:
+        store.wait()
 
 
 def per_device(orbitals, exchange_applied):
@@ -287,8 +342,9 @@
             jax.ShapeDtypeStruct((SETS, NB, width), BF16),
         ),
         in_specs=[anywhere, anywhere],
-        out_specs=(vmem, vmem),
+        out_specs=(vmem, anywhere),
         scratch_shapes=[
+            pltpu.VMEM((SETS, NB, width), BF16),
             pltpu.VMEM((SETS, NB, width), BF16),
             pltpu.VMEM((SETS, GROWS, BLK), F32),
             pltpu.VMEM((SETS, HALF, BLK), F32),
@@ -303,20 +359,25 @@
             pltpu.SemaphoreType.DMA((SETS, 2)),
             pltpu.SemaphoreType.DMA((SETS, 31)),
             pltpu.SemaphoreType.DMA((SETS, 31)),
+            pltpu.SemaphoreType.DMA((SETS,)),
         ],
         compiler_params=pltpu.CompilerParams(collective_id=0, has_side_effects=True, vmem_limit_bytes=VMEM_LIMIT),
     )(orbitals, exchange_applied)
     return pl.pallas_call(
         finish_kernel,
         out_shape=jax.ShapeDtypeStruct((SETS, NB, width), F32),
-        in_specs=[vmem, vmem],
-        out_specs=vmem,
+        in_specs=[vmem, anywhere],
+        out_specs=anywhere,
         scratch_shapes=[
-            pltpu.VMEM((GROWS, BLK), F32),
-            pltpu.VMEM((NB, NB), F32),
-            pltpu.VMEM((BLK, BLK), F32),
-            pltpu.VMEM((BLK, BLK), F32),
-            pltpu.VMEM((BLK, NB), F32),
+            pltpu.VMEM((SETS, GROWS, BLK), F32),
+            pltpu.VMEM((SETS, NB, NB), F32),
+            pltpu.VMEM((BLK, 2 * BLK), F32),
+            pltpu.VMEM((BLK, 2 * BLK), F32),
+            pltpu.VMEM((SETS, BLK, NB), F32),
+            pltpu.VMEM((SETS, NB, width), BF16),
+            pltpu.VMEM((SETS, NB, width), F32),
+            pltpu.SemaphoreType.DMA,
+            pltpu.SemaphoreType.DMA((SETS, NBLK)),
         ],
         compiler_params=pltpu.CompilerParams(vmem_limit_bytes=VMEM_LIMIT),
     )(gram, slab)

time: 198 us -> 179 us (0.904)
  Pallas kernels: 198 us -> 179 us
    pallas_call x1, Pallas kernels: 37.4 us -> 24.1 us  [per_device(): pl.pallas_call(finish_kernel, out_shape=jax.ShapeDtypeStruct((SETS, NB, w...]
    pallas_call x1, Pallas kernels: 161 us -> 154 us  [per_device(): pl.pallas_call(exchange_kernel, out_shape=(jax.ShapeDtypeStruct((SETS, GR...]
where the time goes in v3:
time: 179 us
  Pallas kernels  179 us (100%)
    pallas_call x1, Pallas kernels, per_device(): pl.pallas_call(exchange_kernel, out_shape=(jax.ShapeDtypeStruct((SETS, GR...  154 us
    pallas_call x1, Pallas kernels, per_device(): pl.pallas_call(finish_kernel, out_shape=jax.ShapeDtypeStruct((SETS, NB, w...  24.1 us

profile of v3, /device:TPU:1, one launch (start us, length us, event | category | flops | bytes accessed | tf_op | source)
XLA Modules:
  0.0 178.7 jit_solution(9591503795488537969)
XLA Ops:
  0.0 154.5 %shard_map.28 = (f32[2,1536,128]{2,1,0:T(8,128)}, bf16[2,512,1152]{2,1,0:T(8,128)(2,1)}) custom-call(bf16[2,16,36864]{2,1,0:T(8,128)(2,1)} %o_ref.1, bf16[2,16,36864]{2,1,0:T(8,128)(2,1)} %w_ref.1), custom_call_target="tpu_custom_call" | custom-call | tf_op jit(solution)/shard_map/pallas_call | solution.py:338
  154.5 24.1 %shard_map.29 = f32[2,512,1152]{2,1,0:T(8,128)} custom-call(f32[2,1536,128]{2,1,0:T(8,128)} %get-tuple-element.7.g_ref, bf16[2,512,1152]{2,1,0:T(8,128)(2,1)} %get-tuple-element.8.w_ref), custom_call_target="tpu_custom_call" | custom-call | tf_op jit(solution)/shard_map/pallas_call | solution.py:366

commit v4 on v3

--- a/solution.py
+++ b/solution.py
@@ -8,7 +8,6 @@
 from jax.sharding import PartitionSpec as P
 
 MESH = pl.DeviceIdType.MESH
-HIGHEST = lax.Precision.HIGHEST
 F32 = jnp.float32
 BF16 = jnp.bfloat16
 NB, NG, SETS = 512, 294912, 2
@@ -18,11 +17,18 @@
 PANEL = 16
 PAIRS = [(i, j) for i in range(NBLK) for j in range(i, NBLK)]
 FIRST = [PAIRS.index((i, i)) for i in range(NBLK)]
+USED = len(PAIRS) * BLK
 GROWS = 12 * BLK
+LROWS = 16 * BLK
 XS, YS, ZS = 4, 4, 8
 HALF = GROWS // 2
-PART = HALF // 2 // XS
-CHUNK = 2 * PART // ZS
+PLANES = XS * YS
+CHUNK = HALF // (PLANES + ZS)
+PARTA = CHUNK * ZS
+LHALF = LROWS // 2
+LPLANE = LHALF // PLANES
+LCHUNK = LPLANE // ZS
+MESSAGES = 2 + 3 * (PLANES - 1 + ZS - 1)
 VMEM_LIMIT = 60 * 2**20
 
 def ring(d, n):
@@ -35,12 +41,36 @@
 )
 
 
+PLANE = sorted(
+    [(dy, dx) for dy in range(YS) for dx in range(XS) if (dy, dx) != (0, 0)],
+    key=lambda t: -ring(t[0], YS) - ring(t[1], XS),
+)
+
+
+def pieces(a):
+    head = a.astype(BF16)
+    rest = a - head.astype(F32)
+    middle = rest.astype(BF16)
+    return head, middle, (rest - middle.astype(F32)).astype(BF16)
+
+
+def stacked(left, right, axis_left, axis_right):
+    a, b = pieces(left), pieces(right)
+    order = ((0, 0), (0, 1), (1, 0), (1, 1), (0, 2), (2, 0))
+    return lax.dot_general(
+        jnp.concatenate([a[i] for i, _ in order], axis=axis_left),
+        jnp.concatenate([b[j] for _, j in order], axis=axis_right),
+        (((axis_left,), (axis_right,)), ((), ())),
+        preferred_element_type=F32,
+    )
+
+
 def tn(a, b):
-    return lax.dot_general(a, b, (((0,), (0,)), ((), ())), precision=HIGHEST, preferred_element_type=F32)
+    return stacked(a, b, 0, 0)
 
 
 def nn(a, b):
-    return lax.dot_general(a, b, (((1,), (0,)), ((), ())), precision=HIGHEST, preferred_element_type=F32)
+    return stacked(a, b, 1, 0)
 
 
 def nt(a, b):
@@ -161,7 +191,8 @@
 
 
 def exchange_kernel(
-    o_ref, w_ref, g_out, w_out, o_slab, w_slab, part, half, from_x, from_y, third, from_z, fourth, from_4, send_sem, recv_sem, own_sem, out_sem, in_sem, keep_sem
+    o_ref, w_ref, g_out, w_out, o_slab, w_slab, part, g_sum, half, once, from_a, from_b, then_a, then_b, light, middle, from_p, from_q,
+    send_sem, recv_sem, own_sem, out_sem, in_sem, keep_sem, gram_sem
 ):
     ga, ba = lax.axis_index("ga"), lax.axis_index("ba")
     y, z = ga // ZS, lax.rem(ga, ZS)
@@ -173,11 +204,20 @@
     def ahead(i, k, n):
         return lax.rem(i + k, n)
 
+    def span(start, size):
+        return pl.ds(pl.multiple_of(start, 8), size)
+
     peers = [device(x, ahead(y, dy, YS), ahead(z, dz, ZS), core) for dy, dz in OFFSETS]
     partner = device(x, y, z, 1 - core)
-    beside = [device(ahead(x, k, XS), y, z, core) for k in range(1, XS)]
+    line = [(k, device(x, y, ahead(z, k, ZS), core), ahead(z, k, ZS)) for k in range(1, ZS)]
+    plane = [
+        (dy * XS + dx, device(ahead(x, dx, XS), ahead(y, dy, YS), z, core), ahead(y, dy, YS) * XS + ahead(x, dx, XS))
+        for dy, dx in PLANE
+    ]
+    spot = y * XS + x
+    greeted = [*peers, partner, *(to for (dy, dx), (_, to, _) in zip(PLANE, plane) if dx)]
     barrier = pltpu.get_barrier_semaphore()
-    for p in [*peers, partner, *beside]:
+    for p in greeted:
         pl.semaphore_signal(barrier, inc=1, device_id=p, device_id_type=MESH)
     width = o_slab.shape[2]
     rows = o_ref.shape[1]
@@ -191,8 +231,8 @@
     ]
     for copy in local:
         copy.start()
-    part[:, len(PAIRS) * BLK :, :] = jnp.zeros((SETS, GROWS - len(PAIRS) * BLK, BLK), F32)
-    pl.semaphore_wait(barrier, len(peers) + 1 + len(beside))
+    part[:, USED:, :] = jnp.zeros((SETS, LROWS - USED, BLK), F32)
+    pl.semaphore_wait(barrier, len(greeted))
 
     def send_slabs(s, chosen):
         for p in chosen:
@@ -220,71 +260,65 @@
                 at = (FIRST[i] + j - i) * BLK
                 part[s, at : at + BLK, :] = product[:, (j - i) * BLK : (j - i + 1) * BLK] * (-0.5 / NG)
 
-    def span(start, size):
-        return pl.ds(pl.multiple_of(start, 8), size)
-
-    def total(s, between):
-        used = []
-
-        def stage(t, transfers):
-            copies = []
-            for src, dst, to in transfers:
-                at = len(used) + len(copies)
-                copies.append(
-                    pltpu.make_async_remote_copy(
-                        src_ref=src, dst_ref=dst, send_sem=out_sem.at[s, at], recv_sem=in_sem.at[s, at], device_id=to, device_id_type=MESH
-                    )
-                )
-            for copy in copies:
-                copy.start()
-            between(t)
-            for copy in copies:
-                copy.wait_recv()
-            used.extend(copies)
-
-        stage(0, [(part.at[s, span((1 - core) * HALF, HALF), :], half.at[s], partner)])
-        half[s] = half[s] + part[s, span(core * HALF, HALF), :]
-        side = HALF // 2
-        xs = [ahead(x, k, XS) for k in range(1, XS)]
-        ys = [ahead(y, k, YS) for k in range(1, YS)]
-        zs = [ahead(z, k, ZS) for k in range(1, ZS)]
+    used = [[], []]
+
+    def stage(s, transfers, between=None):
+        copies = [
+            pltpu.make_async_remote_copy(
+                src_ref=src, dst_ref=dst, send_sem=out_sem.at[s, at], recv_sem=in_sem.at[s, at], device_id=to, device_id_type=MESH
+            )
+            for at, (src, dst, to) in enumerate(transfers, len(used[s]))
+        ]
+        for copy in copies:
+            copy.start()
+        if between is not None:
+            send_slabs(1, between)
+        for copy in copies:
+            copy.wait_recv()
+        used[s].extend(copies)
+
+    def added(terms):
+        while len(terms) > 1:
+            terms = [sum(terms[i : i + 2][1:], terms[i]) for i in range(0, len(terms), 2)]
+        return terms[0]
+
+    def total_light(s, batches):
+        stage(s, [(part.at[s, span((1 - core) * LHALF, LHALF), :], light, partner)], batches[0])
+        light[...] = light[...] + part[s, span(core * LHALF, LHALF), :]
+        stage(s, [(light.at[span(i * LPLANE, LPLANE), :], from_p.at[k], to) for k, to, i in plane], batches[1])
+        middle[...] = added([light[span(spot * LPLANE, LPLANE), :]] + [from_p[k] for k in range(1, PLANES)])
+        stage(s, [(middle.at[span(i * LCHUNK, LCHUNK), :], from_q.at[k], to) for k, to, i in line], batches[2])
+        start = core * LHALF + spot * LPLANE
+        here = span(start + z * LCHUNK, LCHUNK)
+        g_sum[s, here, :] = added([middle[span(z * LCHUNK, LCHUNK), :]] + [from_q[k] for k in range(1, ZS)])
+        for batch, done, to_all in (
+            (batches[3], g_sum.at[s, here, :], [to for _, to, _ in line]),
+            (batches[4], g_sum.at[s, span(start, LPLANE), :], [to for _, to, _ in plane]),
+            (batches[5], g_sum.at[s, span(core * LHALF, LHALF), :], [partner]),
+        ):
+            stage(s, [(done, done, to) for to in to_all], batch)
+
+    def total(s):
+        stage(s, [(part.at[s, span((1 - core) * HALF, HALF), :], half, partner)])
+        half[...] = half[...] + part[s, span(core * HALF, HALF), :]
         stage(
-            1,
-            [(half.at[s, span(xx * PART, PART), :], from_x.at[s, k], device(xx, y, z, core)) for k, xx in enumerate(xs)]
-            + [(half.at[s, span(side + yy * PART, PART), :], from_y.at[s, k], device(x, yy, z, core)) for k, yy in enumerate(ys)],
+            s,
+            [(half.at[span(PARTA + i * CHUNK, CHUNK), :], from_b.at[k], to) for k, to, i in plane]
+            + [(half.at[span(i * CHUNK, CHUNK), :], from_a.at[k], to) for k, to, i in line],
         )
-        third[s, :PART, :] = half[s, span(x * PART, PART), :] + (from_x[s, 0] + from_x[s, 1] + from_x[s, 2])
-        third[s, PART:, :] = half[s, span(side + y * PART, PART), :] + (from_y[s, 0] + from_y[s, 1] + from_y[s, 2])
-        stage(2, [(third.at[s, span(zz * CHUNK, CHUNK), :], from_z.at[s, k], device(x, y, zz, core)) for k, zz in enumerate(zs)])
-        got = [from_z[s, k] for k in range(ZS - 1)]
-        fourth[s] = third[s, span(z * CHUNK, CHUNK), :] + (
-            ((got[0] + got[1]) + (got[2] + got[3])) + ((got[4] + got[5]) + got[6])
-        )
-        upper = z // (ZS // 2)
-        stage(
-            3,
-            [
-                (fourth.at[s], from_4.at[s, k - 1], device(ahead(x, k * upper, XS), ahead(y, k * (1 - upper), YS), z, core))
-                for k in range(1, 4)
-            ],
-        )
-        start_x = core * HALF + x * PART
-        start_y = core * HALF + side + y * PART
-        start = (1 - upper) * (start_x + z * CHUNK) + upper * (start_y + (z - ZS // 2) * CHUNK)
-        g_out[s, span(start, CHUNK), :] = fourth[s] + (from_4[s, 0] + from_4[s, 1] + from_4[s, 2])
-        here = g_out.at[s, span(start, CHUNK), :]
-        stage(4, [(here, here, device(x, y, zz, core)) for zz in zs])
-        along_x = g_out.at[s, span(start_x, PART), :]
-        along_y = g_out.at[s, span(start_y, PART), :]
-        stage(
-            5,
-            [(along_x, along_x, device(xx, y, z, core)) for xx in xs] + [(along_y, along_y, device(x, yy, z, core)) for yy in ys],
-        )
-        share = g_out.at[s, span(core * HALF, HALF), :]
-        stage(6, [(share, share, partner)])
-        return used
-
-    cuts = [0, 12, 16, 20, 24, 28, 31, 31, 31]
+        once[0] = added([half[span(z * CHUNK, CHUNK), :]] + [from_a[k] for k in range(1, ZS)])
+        once[1] = added([half[span(PARTA + spot * CHUNK, CHUNK), :]] + [from_b[k] for k in range(1, PLANES)])
+        stage(s, [(once.at[0], then_a.at[k], to) for k, to, _ in plane] + [(once.at[1], then_b.at[k], to) for k, to, _ in line])
+        start_a = span(core * HALF + z * CHUNK, CHUNK)
+        start_b = span(core * HALF + PARTA + spot * CHUNK, CHUNK)
+        g_sum[s, start_a, :] = added([once[0]] + [then_a[k] for k in range(1, PLANES)])
+        g_sum[s, start_b, :] = added([once[1]] + [then_b[k] for k in range(1, ZS)])
+        here_a, here_b = g_sum.at[s, start_a, :], g_sum.at[s, start_b, :]
+        stage(s, [(here_b, here_b, to) for _, to, _ in plane] + [(here_a, here_a, to) for _, to, _ in line])
+        share = g_sum.at[s, span(core * HALF, HALF), :]
+        stage(s, [(share, share, partner)])
+
+    cuts = [0, 12, 16, 20, 24, 28, 31, 31]
     batches = [peers[i:j] for i, j in zip(cuts, cuts[1:])]
     send_slabs(0, peers)
     send_slabs(1, batches[0])
@@ -292,19 +326,22 @@
         copy.wait()
     wait_slabs(0, recv_sem)
     keep = [pltpu.make_async_copy(w_slab.at[s], w_out.at[s], keep_sem.at[s]) for s in range(SETS)]
+    keep_gram = [pltpu.make_async_copy(g_sum.at[s, pl.ds(0, USED), :], g_out.at[s], gram_sem.at[s]) for s in range(SETS)]
     keep[0].start()
     correlate(0)
-    used = total(0, lambda t: send_slabs(1, batches[t + 1]))
+    total_light(0, batches[1:])
+    keep_gram[0].start()
     wait_slabs(1, recv_sem)
     keep[1].start()
     correlate(1)
-    used = used + total(1, lambda t: None)
-    for copy in used:
+    total(1)
+    keep_gram[1].start()
+    for copy in used[0] + used[1]:
         copy.wait_send()
-    for copy in keep:
-        copy.wait()
     for s in range(SETS):
         wait_slabs(s, send_sem)
+    for copy in keep + keep_gram:
+        copy.wait()
 
 
 def finish_kernel(g_ref, w_ref, out_ref, g, x, a, m, u, slab, result, in_sem, out_sem):
@@ -338,27 +375,32 @@
     gram, slab = pl.pallas_call(
         exchange_kernel,
         out_shape=(
-            jax.ShapeDtypeStruct((SETS, GROWS, BLK), F32),
+            jax.ShapeDtypeStruct((SETS, USED, BLK), F32),
             jax.ShapeDtypeStruct((SETS, NB, width), BF16),
         ),
         in_specs=[anywhere, anywhere],
-        out_specs=(vmem, anywhere),
+        out_specs=(anywhere, anywhere),
         scratch_shapes=[
             pltpu.VMEM((SETS, NB, width), BF16),
             pltpu.VMEM((SETS, NB, width), BF16),
-            pltpu.VMEM((SETS, GROWS, BLK), F32),
-            pltpu.VMEM((SETS, HALF, BLK), F32),
-            pltpu.VMEM((SETS, XS - 1, PART, BLK), F32),
-            pltpu.VMEM((SETS, YS - 1, PART, BLK), F32),
-            pltpu.VMEM((SETS, 2 * PART, BLK), F32),
-            pltpu.VMEM((SETS, ZS - 1, CHUNK, BLK), F32),
-            pltpu.VMEM((SETS, CHUNK, BLK), F32),
-            pltpu.VMEM((SETS, 3, CHUNK, BLK), F32),
+            pltpu.VMEM((SETS, LROWS, BLK), F32),
+            pltpu.VMEM((SETS, LROWS, BLK), F32),
+            pltpu.VMEM((HALF, BLK), F32),
+            pltpu.VMEM((2, CHUNK, BLK), F32),
+            pltpu.VMEM((ZS, CHUNK, BLK), F32),
+            pltpu.VMEM((PLANES, CHUNK, BLK), F32),
+            pltpu.VMEM((PLANES, CHUNK, BLK), F32),
+            pltpu.VMEM((ZS, CHUNK, BLK), F32),
+            pltpu.VMEM((LHALF, BLK), F32),
+            pltpu.VMEM((LPLANE, BLK), F32),
+            pltpu.VMEM((PLANES, LPLANE, BLK), F32),
+            pltpu.VMEM((ZS, LCHUNK, BLK), F32),
             pltpu.SemaphoreType.DMA((SETS, 2)),
             pltpu.SemaphoreType.DMA((SETS, 2)),
             pltpu.SemaphoreType.DMA((SETS, 2)),
-            pltpu.SemaphoreType.DMA((SETS, 31)),
-            pltpu.SemaphoreType.DMA((SETS, 31)),
+            pltpu.SemaphoreType.DMA((SETS, MESSAGES)),
+            pltpu.SemaphoreType.DMA((SETS, MESSAGES)),
+            pltpu.SemaphoreType.DMA((SETS,)),
             pltpu.SemaphoreType.DMA((SETS,)),
         ],
         compiler_params=pltpu.CompilerParams(collective_id=0, has_side_effects=True, vmem_limit_bytes=VMEM_LIMIT),
@@ -369,7 +411,7 @@
         in_specs=[vmem, anywhere],
         out_specs=anywhere,
         scratch_shapes=[
-            pltpu.VMEM((SETS, GROWS, BLK), F32),
+            pltpu.VMEM((SETS, USED, BLK), F32),
             pltpu.VMEM((SETS, NB, NB), F32),
             pltpu.VMEM((BLK, 2 * BLK), F32),
             pltpu.VMEM((BLK, 2 * BLK), F32),

time: 179 us -> 167 us (0.933)
  Pallas kernels: 179 us -> 166 us
    pallas_call x1, Pallas kernels: 154 us -> 146 us  [per_device(): pl.pallas_call(exchange_kernel, out_shape=(jax.ShapeDtypeStruct((SETS, US...]
    pallas_call x1, Pallas kernels: 24.1 us -> 20.3 us  [per_device(): pl.pallas_call(finish_kernel, out_shape=jax.ShapeDtypeStruct((SETS, NB, w...]
where the time goes in v4:
time: 167 us
  Pallas kernels  166 us (99%)
    pallas_call x1, Pallas kernels, per_device(): pl.pallas_call(exchange_kernel, out_shape=(jax.ShapeDtypeStruct((SETS, US...  146 us
    pallas_call x1, Pallas kernels, per_device(): pl.pallas_call(finish_kernel, out_shape=jax.ShapeDtypeStruct((SETS, NB, w...  20.3 us

profile of v4, /device:TPU:1, one launch (start us, length us, event | category | flops | bytes accessed | tf_op | source)
XLA Modules:
  0.0 166.5 jit_solution(4552468688229318753)
XLA Ops:
  0.0 146.0 %shard_map.28 = (f32[2,1280,128]{2,1,0:T(8,128)}, bf16[2,512,1152]{2,1,0:T(8,128)(2,1)}) custom-call(bf16[2,16,36864]{2,1,0:T(8,128)(2,1)} %o_ref.1, bf16[2,16,36864]{2,1,0:T(8,128)(2,1)} %w_ref.1), custom_call_target="tpu_custom_call" | custom-call | tf_op jit(solution)/shard_map/pallas_call | solution.py:375
  146.0 20.3 %shard_map.29 = f32[2,512,1152]{2,1,0:T(8,128)} custom-call(f32[2,1280,128]{2,1,0:T(8,128)} %get-tuple-element.7.g_ref, bf16[2,512,1152]{2,1,0:T(8,128)(2,1)} %get-tuple-element.8.w_ref), custom_call_target="tpu_custom_call" | custom-call | tf_op jit(solution)/shard_map/pallas_call | solution.py:408

commit v5 on v4

--- a/solution.py
+++ b/solution.py
@@ -29,7 +29,7 @@
 LPLANE = LHALF // PLANES
 LCHUNK = LPLANE // ZS
 MESSAGES = 2 + 3 * (PLANES - 1 + ZS - 1)
-VMEM_LIMIT = 60 * 2**20
+VMEM_LIMIT = 50 * 2**20
 
 def ring(d, n):
     return min(d, n - d)
@@ -171,28 +171,34 @@
             @pl.when(k == kk)
             def _():
                 lo, hi = BLK * kk, BLK * kk + BLK
+                below = NB - hi
                 for s, m in enumerate(ms):
+                    x_ref[s, lo:hi, lo:hi] = m
+                    right = [g_ref[s, block(kk, j), :] for j in range(kk + 1, NBLK)]
+                    left = [x_ref[s, lo:hi, :lo]] if kk else []
+                    row = nn(m, jnp.concatenate(right + left, axis=1))
+                    if below:
+                        u_ref[s, :, hi:] = row[:, :below]
                     if kk:
-                        x_ref[s, lo:hi, :lo] = nn(m, x_ref[s, lo:hi, :lo])
-                    x_ref[s, lo:hi, lo:hi] = m
-                    for j in range(kk + 1, NBLK):
-                        u_ref[s, :, j * BLK : (j + 1) * BLK] = nn(m, g_ref[s, block(kk, j), :])
-                for s, m in enumerate(ms):
-                    for i in range(kk + 1, NBLK):
-                        li = BLK * i
-                        ui = u_ref[s, :, li : li + BLK]
-                        update = tn(ui, u_ref[s, :, li:])
-                        for j in range(i, NBLK):
-                            g_ref[s, block(i, j), :] = g_ref[s, block(i, j), :] - update[:, (j - i) * BLK : (j - i + 1) * BLK]
-                        x_ref[s, li : li + BLK, :hi] = x_ref[s, li : li + BLK, :hi] - tn(ui, x_ref[s, lo:hi, :hi])
+                        x_ref[s, lo:hi, :lo] = row[:, below:]
+                if below:
+                    for s in range(SETS):
+                        u = u_ref[s, :, hi:]
+                        update = nn(u.T, jnp.concatenate([u, x_ref[s, lo:hi, :hi]], axis=1))
+                        for i in range(kk + 1, NBLK):
+                            at = slice(BLK * i - hi, BLK * i - hi + BLK)
+                            for j in range(i, NBLK):
+                                g_ref[s, block(i, j), :] = g_ref[s, block(i, j), :] - update[at, BLK * j - hi : BLK * j - hi + BLK]
+                            li = BLK * i
+                            x_ref[s, li : li + BLK, :hi] = x_ref[s, li : li + BLK, :hi] - update[at, below:]
         return carry
 
     lax.fori_loop(0, NBLK, step, 0)
 
 
 def exchange_kernel(
-    o_ref, w_ref, g_out, w_out, o_slab, w_slab, part, g_sum, half, once, from_a, from_b, then_a, then_b, light, middle, from_p, from_q,
-    send_sem, recv_sem, own_sem, out_sem, in_sem, keep_sem, gram_sem
+    o_ref, w_ref, g_sum, w_out, o_slab, w_slab, part, half, once, from_a, from_b, then_a, then_b, light, middle, from_p, from_q,
+    send_sem, recv_sem, own_sem, out_sem, in_sem, keep_sem
 ):
     ga, ba = lax.axis_index("ga"), lax.axis_index("ba")
     y, z = ga // ZS, lax.rem(ga, ZS)
@@ -253,12 +259,14 @@
             pltpu.make_async_copy(all_but_one, all_but_one, sem.at[s, a]).wait()
 
     def correlate(s):
-        for i in range(NBLK):
-            lo = BLK * i
-            product = nt(o_slab[s, lo : lo + BLK, :], w_slab[s, lo:, :]) + nt(w_slab[s, lo : lo + BLK, :], o_slab[s, lo:, :])
-            for j in range(i, NBLK):
-                at = (FIRST[i] + j - i) * BLK
-                part[s, at : at + BLK, :] = product[:, (j - i) * BLK : (j - i + 1) * BLK] * (-0.5 / NG)
+        for i in range(0, NBLK, 2):
+            lo, hi = BLK * i, BLK * (i + 2)
+            product = nt(o_slab[s, lo:hi, :], w_slab[s, lo:, :]) + nt(w_slab[s, lo:hi, :], o_slab[s, lo:, :])
+            for k in range(i, i + 2):
+                for j in range(k, NBLK):
+                    at = (FIRST[k] + j - k) * BLK
+                    block = product[(k - i) * BLK : (k - i + 1) * BLK, (j - i) * BLK : (j - i + 1) * BLK]
+                    part[s, at : at + BLK, :] = block * (-0.5 / NG)
 
     used = [[], []]
 
@@ -326,43 +334,39 @@
         copy.wait()
     wait_slabs(0, recv_sem)
     keep = [pltpu.make_async_copy(w_slab.at[s], w_out.at[s], keep_sem.at[s]) for s in range(SETS)]
-    keep_gram = [pltpu.make_async_copy(g_sum.at[s, pl.ds(0, USED), :], g_out.at[s], gram_sem.at[s]) for s in range(SETS)]
     keep[0].start()
     correlate(0)
     total_light(0, batches[1:])
-    keep_gram[0].start()
     wait_slabs(1, recv_sem)
     keep[1].start()
     correlate(1)
     total(1)
-    keep_gram[1].start()
     for copy in used[0] + used[1]:
         copy.wait_send()
     for s in range(SETS):
         wait_slabs(s, send_sem)
-    for copy in keep + keep_gram:
+    for copy in keep:
         copy.wait()
 
 
 def finish_kernel(g_ref, w_ref, out_ref, g, x, a, m, u, slab, result, in_sem, out_sem):
     fetch = pltpu.make_async_copy(w_ref, slab, in_sem)
     fetch.start()
-    g[...] = g_ref[...]
+    g[...] = g_ref[:, :USED, :]
     factor(g, x, a, m, u)
     fetch.wait()
     stores = []
+    tall = 2 * BLK
     for s in range(SETS):
-        for i in range(NBLK):
-            lo, hi = BLK * i, BLK * i + BLK
+        for i in range(NB // tall):
+            lo, hi = tall * i, tall * i + tall
             inverse = x[s, lo:hi, :hi]
             head = inverse.astype(BF16)
             tail = (inverse - head.astype(F32)).astype(BF16)
-            known = slab[s, :hi, :]
-            result[s, lo:hi, :] = jnp.dot(head, known, preferred_element_type=F32) + jnp.dot(
-                tail, known, preferred_element_type=F32
-            )
-            here = result.at[s, pl.ds(lo, BLK), :]
-            stores.append(pltpu.make_async_copy(here, out_ref.at[s, pl.ds(lo, BLK), :], out_sem.at[s, i]))
+            both = jnp.dot(jnp.concatenate([head, tail], axis=0), slab[s, :hi, :], preferred_element_type=F32)
+            result[s, lo:hi, :] = both[:tall] + both[tall:]
+            here = result.at[s, pl.ds(lo, tall), :]
+            stores.append(pltpu.make_async_copy(here, out_ref.at[s, pl.ds(lo, tall), :], out_sem.at[s, i]))
             stores[-1].start()
     for store in stores:
         store.wait()
@@ -375,15 +379,14 @@
     gram, slab = pl.pallas_call(
         exchange_kernel,
         out_shape=(
-            jax.ShapeDtypeStruct((SETS, USED, BLK), F32),
+            jax.ShapeDtypeStruct((SETS, LROWS, BLK), F32),
             jax.ShapeDtypeStruct((SETS, NB, width), BF16),
         ),
         in_specs=[anywhere, anywhere],
-        out_specs=(anywhere, anywhere),
+        out_specs=(vmem, anywhere),
         scratch_shapes=[
             pltpu.VMEM((SETS, NB, width), BF16),
             pltpu.VMEM((SETS, NB, width), BF16),
-            pltpu.VMEM((SETS, LROWS, BLK), F32),
             pltpu.VMEM((SETS, LROWS, BLK), F32),
             pltpu.VMEM((HALF, BLK), F32),
             pltpu.VMEM((2, CHUNK, BLK), F32),
@@ -400,7 +403,6 @@
             pltpu.SemaphoreType.DMA((SETS, 2)),
             pltpu.SemaphoreType.DMA((SETS, MESSAGES)),
             pltpu.SemaphoreType.DMA((SETS, MESSAGES)),
-            pltpu.SemaphoreType.DMA((SETS,)),
             pltpu.SemaphoreType.DMA((SETS,)),
         ],
         compiler_params=pltpu.CompilerParams(collective_id=0, has_side_effects=True, vmem_limit_bytes=VMEM_LIMIT),

time: 167 us -> 163 us (0.976)
  Pallas kernels: 166 us -> 163 us
    pallas_call x1, Pallas kernels: 146 us -> 144 us  [per_device(): pl.pallas_call(exchange_kernel, out_shape=(jax.ShapeDtypeStruct((SETS, LR...]
where the time goes in v5:
time: 163 us
  Pallas kernels  163 us (100%)
    pallas_call x1, Pallas kernels, per_device(): pl.pallas_call(exchange_kernel, out_shape=(jax.ShapeDtypeStruct((SETS, LR...  144 us
    pallas_call x1, Pallas kernels, per_device(): pl.pallas_call(finish_kernel, out_shape=jax.ShapeDtypeStruct((SETS, NB, w...  19 us

profile of v5, /device:TPU:1, one launch (start us, length us, event | category | flops | bytes accessed | tf_op | source)
XLA Modules:
  0.0 163.4 jit_solution(8562686239675305167)
XLA Ops:
  0.0 144.3 %shard_map.28 = (f32[2,2048,128]{2,1,0:T(8,128)S(1)}, bf16[2,512,1152]{2,1,0:T(8,128)(2,1)}) custom-call(bf16[2,16,36864]{2,1,0:T(8,128)(2,1)} %o_ref.1, bf16[2,16,36864]{2,1,0:T(8,128)(2,1)} %w_ref.1), custom_call_target="tpu_custom_call" | custom-call | tf_op jit(solution)/shard_map/pallas_call | solution.py:379
  144.3 19.0 %shard_map.29 = f32[2,512,1152]{2,1,0:T(8,128)} custom-call(f32[2,2048,128]{2,1,0:T(8,128)S(1)} %get-tuple-element.7.g_ref, bf16[2,512,1152]{2,1,0:T(8,128)(2,1)} %get-tuple-element.8.w_ref), custom_call_target="tpu_custom_call" | custom-call | tf_op jit(solution)/shard_map/pallas_call | solution.py:410

commit v6 on v5

--- a/solution.py
+++ b/solution.py
@@ -18,13 +18,14 @@
 PAIRS = [(i, j) for i in range(NBLK) for j in range(i, NBLK)]
 FIRST = [PAIRS.index((i, i)) for i in range(NBLK)]
 USED = len(PAIRS) * BLK
-GROWS = 12 * BLK
+GROWS = USED
 LROWS = 16 * BLK
 XS, YS, ZS = 4, 4, 8
 HALF = GROWS // 2
 PLANES = XS * YS
-CHUNK = HALF // (PLANES + ZS)
-PARTA = CHUNK * ZS
+CHUNKA = 32
+PARTA = CHUNKA * ZS
+CHUNKB = (HALF - PARTA) // PLANES
 LHALF = LROWS // 2
 LPLANE = LHALF // PLANES
 LCHUNK = LPLANE // ZS
@@ -311,16 +312,16 @@
         half[...] = half[...] + part[s, span(core * HALF, HALF), :]
         stage(
             s,
-            [(half.at[span(PARTA + i * CHUNK, CHUNK), :], from_b.at[k], to) for k, to, i in plane]
-            + [(half.at[span(i * CHUNK, CHUNK), :], from_a.at[k], to) for k, to, i in line],
+            [(half.at[span(PARTA + i * CHUNKB, CHUNKB), :], from_b.at[k], to) for k, to, i in plane]
+            + [(half.at[span(i * CHUNKA, CHUNKA), :], from_a.at[k], to) for k, to, i in line],
         )
-        once[0] = added([half[span(z * CHUNK, CHUNK), :]] + [from_a[k] for k in range(1, ZS)])
-        once[1] = added([half[span(PARTA + spot * CHUNK, CHUNK), :]] + [from_b[k] for k in range(1, PLANES)])
-        stage(s, [(once.at[0], then_a.at[k], to) for k, to, _ in plane] + [(once.at[1], then_b.at[k], to) for k, to, _ in line])
-        start_a = span(core * HALF + z * CHUNK, CHUNK)
-        start_b = span(core * HALF + PARTA + spot * CHUNK, CHUNK)
+        once[0] = added([half[span(z * CHUNKA, CHUNKA), :]] + [from_a[k] for k in range(1, ZS)])
+        once[1, :CHUNKB] = added([half[span(PARTA + spot * CHUNKB, CHUNKB), :]] + [from_b[k] for k in range(1, PLANES)])
+        stage(s, [(once.at[0], then_a.at[k], to) for k, to, _ in plane] + [(once.at[1, pl.ds(0, CHUNKB), :], then_b.at[k], to) for k, to, _ in line])
+        start_a = span(core * HALF + z * CHUNKA, CHUNKA)
+        start_b = span(core * HALF + PARTA + spot * CHUNKB, CHUNKB)
         g_sum[s, start_a, :] = added([once[0]] + [then_a[k] for k in range(1, PLANES)])
-        g_sum[s, start_b, :] = added([once[1]] + [then_b[k] for k in range(1, ZS)])
+        g_sum[s, start_b, :] = added([once[1, :CHUNKB]] + [then_b[k] for k in range(1, ZS)])
         here_a, here_b = g_sum.at[s, start_a, :], g_sum.at[s, start_b, :]
         stage(s, [(here_b, here_b, to) for _, to, _ in plane] + [(here_a, here_a, to) for _, to, _ in line])
         share = g_sum.at[s, span(core * HALF, HALF), :]
@@ -389,11 +390,11 @@
             pltpu.VMEM((SETS, NB, width), BF16),
             pltpu.VMEM((SETS, LROWS, BLK), F32),
             pltpu.VMEM((HALF, BLK), F32),
-            pltpu.VMEM((2, CHUNK, BLK), F32),
-            pltpu.VMEM((ZS, CHUNK, BLK), F32),
-            pltpu.VMEM((PLANES, CHUNK, BLK), F32),
-            pltpu.VMEM((PLANES, CHUNK, BLK), F32),
-            pltpu.VMEM((ZS, CHUNK, BLK), F32),
+            pltpu.VMEM((2, CHUNKA, BLK), F32),
+            pltpu.VMEM((ZS, CHUNKA, BLK), F32),
+            pltpu.VMEM((PLANES, CHUNKB, BLK), F32),
+            pltpu.VMEM((PLANES, CHUNKA, BLK), F32),
+            pltpu.VMEM((ZS, CHUNKB, BLK), F32),
             pltpu.VMEM((LHALF, BLK), F32),
             pltpu.VMEM((LPLANE, BLK), F32),
             pltpu.VMEM((PLANES, LPLANE, BLK), F32),

time: 163 us -> 163 us (level)
  no operation moved by 1% of the time
where the time goes in v6:
time: 163 us
  Pallas kernels  163 us (100%)
    pallas_call x1, Pallas kernels, per_device(): pl.pallas_call(exchange_kernel, out_shape=(jax.ShapeDtypeStruct((SETS, LR...  144 us
    pallas_call x1, Pallas kernels, per_device(): pl.pallas_call(finish_kernel, out_shape=jax.ShapeDtypeStruct((SETS, NB, w...  18.8 us

profile of v6, /device:TPU:1, one launch (start us, length us, event | category | flops | bytes accessed | tf_op | source)
XLA Modules:
  0.0 162.6 jit_solution(9199050373163383112)
XLA Ops:
  0.0 143.8 %shard_map.28 = (f32[2,2048,128]{2,1,0:T(8,128)S(1)}, bf16[2,512,1152]{2,1,0:T(8,128)(2,1)}) custom-call(bf16[2,16,36864]{2,1,0:T(8,128)(2,1)} %o_ref.1, bf16[2,16,36864]{2,1,0:T(8,128)(2,1)} %w_ref.1), custom_call_target="tpu_custom_call" | custom-call | tf_op jit(solution)/shard_map/pallas_call | solution.py:380
  143.8 18.8 %shard_map.29 = f32[2,512,1152]{2,1,0:T(8,128)} custom-call(f32[2,2048,128]{2,1,0:T(8,128)S(1)} %get-tuple-element.7.g_ref, bf16[2,512,1152]{2,1,0:T(8,128)(2,1)} %get-tuple-element.8.w_ref), custom_call_target="tpu_custom_call" | custom-call | tf_op jit(solution)/shard_map/pallas_call | solution.py:411
